TPU v7x, 32 devices: a whole 2x2x4 slice. The times are simulated.
32 devices in a mesh: group: 2 (over x), dp: 16 (over z, y, core).
Axes of the slice: x: 2, y: 2, z: 4, core: 2. Of those that a mesh axis runs over, the one named last changes fastest.
Arguments:
- hidden_in: bfloat16 [1024, 5120], P('group', 'dp'), parts along dimension 0, may hold values from -6 to 6
- w_gate: bfloat16 [5120, 13824], P(None, 'dp'), may hold values from -0.078125 to 0.078125
- w_up: bfloat16 [5120, 13824], P(None, 'dp'), may hold values from -0.078125 to 0.078125
- w_down: bfloat16 [13824, 5120], P('dp'), may hold values from -0.0546875 to 0.0546875
- norm_gain: float32 [5120], replicated, may hold values from 0.25 to 1.75
- out_cotangent: bfloat16 [1024, 5120], P('group', 'dp'), parts along dimension 0, may hold values from -6 to 6
- proj_model: bfloat16 [3, 64, 5120], replicated, may hold values from -0.078125 to 0.078125
- proj_hidden: bfloat16 [3, 64, 13824], P(None, None, 'dp'), may hold values from -0.0546875 to 0.0546875
- queries: bfloat16 [1024, 12288], P('dp'), may hold values from -0.0546875 to 0.0546875
Outputs:
- block_out: bfloat16 [1024, 5120], P('group', 'dp'), parts along dimension 0
- scores: float32 [4, 1024], P('group', 'dp'), parts along dimension 0
There are 2 independent parts, one for each index of `group`. A program takes and returns all parts, laid end to end along the dimension named above; an argument that names none is the same for every part. Nothing has to cross between parts.
All inputs are finite; a program needn't handle non-finite values.
Results may differ from a plain program's by a relative error of at most 0.005.
Values may be sent and summed in bfloat16 or wider, within the bound.
A program may use at most 128 MiB of HBM per device.

v0:
```python
import jax
import jax.numpy as jnp
from jax import lax
from jax.sharding import PartitionSpec as P

SEQ = 256


epsilon = 1e-06


def contract_last(left_mat, right_mat):
    return lax.dot_general(
        left_mat, right_mat, (((1,), (1,)), ((), ())), preferred_element_type=jnp.float32
    )


def contract_lead(left_mat, right_mat):
    return lax.dot_general(
        left_mat, right_mat, (((0,), (1,)), ((), ())), preferred_element_type=jnp.float32
    )


def pair_sketch(inputs_side, grads_side, seq_count):
    inputs_seq = inputs_side.reshape(seq_count, SEQ, inputs_side.shape[1])
    grads_seq = grads_side.reshape(seq_count, SEQ, grads_side.shape[1])
    return jnp.einsum("stk,stj->skj", inputs_seq, grads_seq, precision=lax.Precision.HIGHEST)


def on_device(
    hidden_in, w_gate, w_up, w_down, norm_gain, out_cotangent, proj_model, proj_hidden, queries
):
    width_cols = hidden_in.shape[1]
    rank = proj_model.shape[1]
    devices = lax.axis_size("dp")
    width = width_cols * devices
    total_rows = hidden_in.shape[0]
    seq_count = total_rows // SEQ
    in_sides = proj_model[0:2].reshape(2 * rank, width)
    out_side = proj_model[2]
    first_col = lax.axis_index("dp") * width_cols
    piece = lax.all_gather(hidden_in, "dp", axis=1, tiled=True)
    gate_value = jnp.dot(piece, w_gate, preferred_element_type=jnp.float32)
    up_value = jnp.dot(piece, w_up, preferred_element_type=jnp.float32)
    projected = contract_last(piece, in_sides)
    in_gate = projected[:, :rank]
    in_up = projected[:, rank:]
    sigmoid_gate = jax.nn.sigmoid(gate_value)
    activated = gate_value * sigmoid_gate
    hidden = (activated * up_value).astype(jnp.bfloat16)
    down_cols = lax.psum_scatter(
        contract_lead(w_down, hidden), "dp", scatter_dimension=0, tiled=True
    )
    gain_cols = lax.dynamic_slice_in_dim(norm_gain, first_col, width_cols, 0)[:, None]
    scaled = gain_cols * jnp.transpose(out_cotangent).astype(jnp.float32)
    square_sums, mixed_sums = lax.psum(
        (jnp.sum(down_cols * down_cols, axis=0), jnp.sum(scaled * down_cols, axis=0)), "dp"
    )
    inv_rms = lax.rsqrt(square_sums / width + epsilon)[None, :]
    mixed_mean = (mixed_sums / width)[None, :]
    block_out = (
        hidden_in.astype(jnp.float32) + jnp.transpose(down_cols * inv_rms * gain_cols)
    ).astype(jnp.bfloat16)
    grad_cols = (inv_rms * (scaled - down_cols * inv_rms * inv_rms * mixed_mean)).astype(
        jnp.bfloat16
    )
    block_cols = lax.all_gather(grad_cols, "dp", axis=0, tiled=True)
    grad_hidden = contract_lead(block_cols, w_down)
    out_down = contract_lead(block_cols, out_side)
    grad_up = (grad_hidden * activated).astype(jnp.bfloat16)
    grad_gate = (
        grad_hidden * up_value * sigmoid_gate * (1.0 + gate_value * (1.0 - sigmoid_gate))
    ).astype(jnp.bfloat16)
    out_gate = contract_last(grad_gate, proj_hidden[0])
    out_up = contract_last(grad_up, proj_hidden[1])
    in_down = contract_last(hidden, proj_hidden[2])
    out_gate, out_up, in_down = lax.psum((out_gate, out_up, in_down), "dp")
    sketch = jnp.stack(
        [
            pair_sketch(in_gate, out_gate, seq_count),
            pair_sketch(in_up, out_up, seq_count),
            pair_sketch(in_down, out_down, seq_count),
        ],
        axis=1,
    )
    flat = sketch.reshape(seq_count, 3 * rank * rank)
    scores = jnp.dot(flat, queries.astype(jnp.float32).T, precision=lax.Precision.HIGHEST)
    return (block_out, scores)


def solution(mesh):
    in_specs = (
        P("group", "dp"),
        P(None, "dp"),
        P(None, "dp"),
        P("dp", None),
        P(),
        P("group", "dp"),
        P(),
        P(None, None, "dp"),
        P("dp", None),
    )
    out_specs = (P("group", "dp"), P("group", "dp"))
    return jax.shard_map(
        on_device, mesh=mesh, in_specs=in_specs, out_specs=out_specs, check_vma=False
    )
```

profile of v0, /device:TPU:0, one launch (start us, length us, event | category | flops | bytes accessed | tf_op | source)
XLA Modules:
  0.0 437.6 jit_solution(17920204076941602003)
XLA Ops:
  7.2 0.7 all-gather.3.cloned.1.call-update
  8.0 61.1 %all-gather.3.cloned.1.call-done = bf16[512,5120]{0,1:T(8,128)(2,1)} async-done(((bf16[512,320]{0,1:T(8,128)(2,1)}), bf16[512,5120]{0,1:T(8,128)(2,1)}) %all-gather.3.cloned.1.call-update) | async-done | bytes 5242896 | tf_op jit(solution)/shard_map/all_gather | solution.py:42
  69.0 8.9 %fusion.26 = f32[512,864]{0,1:T(8,128)S(1)} fusion(bf16[5120,864]{0,1:T(8,128)(2,1)} %param.10, bf16[512,5120]{0,1:T(8,128)(2,1)} %all-gather.3.cloned.1.call-done), kind=kOutput, calls=%fused_computation.44 | convolution fusion | flops 4529848320 | bytes 15859712 | tf_op jit(solution)/shard_map/dot_general | solution.py:43
  77.9 10.3 %multiply_convert_fusion.2 = (bf16[512,864]{0,1:T(8,128)(2,1)S(1)}, f32[512,864]{0,1:T(8,128)}) fusion(f32[512,864]{0,1:T(8,128)S(1)} %fusion.26, bf16[5120,864]{0,1:T(8,128)(2,1)} %param.11, bf16[512,5120]{0,1:T(8,128)(2,1)S(1)} %copy-done.2), kind=kOutput, calls=%fused_computation.3 | convolution fusion | flops 4532502528 | bytes 18513920 | tf_op jit(solution)/shard_map/dot_general | solution.py:44
  88.2 0.9 copy-done.4
  89.1 8.3 %convolution_bitcast_fusion = f32[5120,512]{0,1:T(8,128)} fusion(bf16[512,864]{0,1:T(8,128)(2,1)S(1)} %get-tuple-element.15, bf16[864,5120]{1,0:T(8,128)(2,1)S(1)} %bitcast.80), kind=kOutput, calls=%fused_computation | convolution fusion | flops 4529848320 | bytes 20217856 | tf_op jit(solution)/shard_map/dot_general | solution.py:19
  97.5 11.4 %copy.48 = f32[5120,512]{1,0:T(8,128)} copy(f32[5120,512]{0,1:T(8,128)} %convolution_bitcast_fusion) | data formatting | bytes 20971520
  109.0 0.8 dynamic_slice.3
  109.8 116.9 %reduce-scatter.4.cloned.1.call-done = f32[320,512]{1,0:T(8,128)} async-done(((f32[5120,512]{1,0:T(8,128)}), f32[320,512]{1,0:T(8,128)}) %reduce-scatter.4.cloned.1.call-update) | async-done | bytes 655376 | tf_op jit(solution)/shard_map/reduce_scatter | solution.py:51
  226.7 1.4 copy.49
  228.4 32.2 %all-reduce = (f32[512]{0:T(512)S(1)}, f32[512]{0:T(512)S(1)}) all-reduce(f32[512]{0:T(512)S(1)} %multiply_reduce_fusion, f32[512]{0:T(512)S(1)} %fusion.5), channel_id=1, replica_groups=mesh['group'=2,'dp'=16] {'dp'}, use_global_device_ids=true, to_apply=%region_2.0 | all-reduce | flops 1024 | bytes 8192 | tf_op jit(solution)/shard_map/psum | solution.py:56
  260.6 0.9 fusion.7
  261.8 1.3 copy-done.5
  263.1 1.2 fusion.15
  264.3 0.7 copy.66
  265.0 3.6 fusion.27
  268.6 0.7 fusion.24
  269.3 0.9 fusion.8
  270.2 44.8 %all-gather.5.cloned.1.call-done = bf16[5120,512]{1,0:T(8,128)(2,1)} async-done(((bf16[320,512]{1,0:T(8,128)(2,1)}), bf16[5120,512]{1,0:T(8,128)(2,1)}) %all-gather.5.cloned.1.call-update) | async-done | bytes 5242896 | tf_op jit(solution)/shard_map/all_gather | solution.py:67
  315.0 8.8 %fusion.28 = f32[512,864]{0,1:T(8,128)S(1)} fusion(bf16[864,5120]{1,0:T(8,128)(2,1)} %param.12, bf16[5120,512]{1,0:T(8,128)(2,1)} %all-gather.5.cloned.1.call-done), kind=kOutput, calls=%fused_computation.46 | convolution fusion | flops 4529848320 | bytes 15859712 | tf_op jit(solution)/shard_map/dot_general | solution.py:19
  323.9 0.6 fusion.1
  324.5 0.8 copy-done.11
  325.3 0.8 fusion.2
  326.2 0.7 copy.67
  326.8 0.6 copy.68
  327.5 7.9 %copy.46 = bf16[512,5120]{1,0:T(8,128)(2,1)} copy(bf16[512,5120]{0,1:T(8,128)(2,1)} %bitcast.81) | data formatting | bytes 10485760 | tf_op jit(solution)/shard_map/dot_general | solution.py:19
  335.4 4.8 %fusion.3 = f32[2,256,64]{1,2,0:T(8,128)} fusion(bf16[2,256,5120]{2,1,0:T(8,128)(2,1)} %bitcast.78, bf16[3,64,5120]{2,1,0:T(8,128)(2,1)S(1)} %copy-done.3), kind=kOutput, calls=%fused_computation.12 | convolution fusion | flops 335544320 | bytes 6029312 | tf_op jit(solution)/shard_map/dot_general | solution.py:19
  340.2 85.0 %all-reduce.4.cloned.1.call-done = (f32[2,256,64]{1,2,0:T(8,128)}, f32[2,256,64]{1,2,0:T(8,128)}, f32[2,256,64]{1,2,0:T(8,128)}) async-done(((f32[2,256,64]{1,2,0:T(8,128)}, f32[2,256,64]{1,2,0:T(8,128)}, f32[2,256,64]{1,2,0:T(8,128)}), (f32[2,256,64]{1,2,0:T(8,128)}, f32[2,256,64]{1,2,0:T(8,128)}, f32[2,256,64]{1,2,0:T(8,128)})) %all-reduce.4.cloned.1.call-update) | async-done | bytes 393232 | tf_op jit(solution)/shard_map/psum | solution.py:77
  425.2 1.2 convolution_bitcast_fusion.3
  426.5 1.2 convolution_bitcast_fusion.2
  427.7 1.2 convolution_bitcast_fusion.1
  429.1 1.9 fusion.25
  (43 shorter events, 0.9 us)
Async XLA Ops:
  7.2 422.0 %copy-start = (bf16[64,12288]{1,0:T(8,128)(2,1)S(1)}, bf16[64,12288]{1,0:T(8,128)(2,1)}, u32[]{:S(2)}) copy-start(bf16[64,12288]{1,0:T(8,128)(2,1)} %param.17) | copy-start | bytes 4718596
  7.2 61.8 %all-gather.3.cloned.1.call-start = ((), (), s32[]{:S(2)}) async-start(), calls=%async_computation.1 | async-start | bytes 5570560 | tf_op jit(solution)/shard_map/all_gather | solution.py:42
  7.9 218.8 %reduce-scatter.4.cloned.1.call-start = ((), (), s32[]{:S(2)}) async-start(), calls=%async_computation.3 | async-start | bytes 11141120 | tf_op jit(solution)/shard_map/reduce_scatter | solution.py:51
  69.0 8.9 %copy-start.2 = (bf16[512,5120]{0,1:T(8,128)(2,1)S(1)}, bf16[512,5120]{0,1:T(8,128)(2,1)}, u32[]{:S(2)}) copy-start(bf16[512,5120]{0,1:T(8,128)(2,1)} %all-gather.3.cloned.1.call-done) | copy-start | bytes 15728644
  69.0 20.1 %slice-start = ((s8[8847360]{0:T(1024)(128)(4,1)}), s8[4194304]{0:T(1024)(128)(4,1)S(1)}, s32[]{:S(2)}) async-start(s8[8847360]{0:T(1024)(128)(4,1)} %bitcast.79), calls=%async_computation.5 | async-start | bytes 8388608
  69.0 20.1 %slice-start.1 = ((s8[8847360]{0:T(1024)(128)(4,1)}), s8[4194304]{0:T(1024)(128)(4,1)S(1)}, s32[]{:S(2)}) async-start(s8[8847360]{0:T(1024)(128)(4,1)} %bitcast.79), calls=%async_computation.6 | async-start | bytes 8388608
  77.9 10.3 %copy-start.9 = (f32[512,864]{0,1:T(8,128)}, f32[512,864]{0,1:T(8,128)S(1)}, u32[]{:S(2)}) copy-start(f32[512,864]{0,1:T(8,128)S(1)} %fusion.26) | copy-start | bytes 5308420
  77.9 11.2 %slice-start.2 = ((s8[8847360]{0:T(1024)(128)(4,1)}), s8[458752]{0:T(1024)(128)(4,1)S(1)}, s32[]{:S(2)}) async-start(s8[8847360]{0:T(1024)(128)(4,1)} %bitcast.79), calls=%async_computation.7 | async-start | bytes 917504
  88.2 0.9 copy-start.4
  108.9 119.3 %copy-start.7 = (bf16[512,320]{0,1:T(8,128)(2,1)S(1)}, bf16[512,320]{0,1:T(8,128)(2,1)}, u32[]{:S(2)}) copy-start(bf16[512,320]{0,1:T(8,128)(2,1)} %param.14) | copy-start | bytes 983044
  108.9 206.1 %all-gather.5.cloned.1.call-start = ((), (), s32[]{:S(2)}) async-start(), calls=%async_computation.2 | async-start | bytes 5570560 | tf_op jit(solution)/shard_map/all_gather | solution.py:67
  226.7 1.6 copy-start.1
  261.6 3.4 slice-start.3
  261.6 163.6 %all-reduce.4.cloned.1.call-start = ((), (), s32[]{:S(2)}) async-start(), calls=%async_computation.4 | async-start | bytes 786432 | tf_op jit(solution)/shard_map/psum | solution.py:77
  261.8 1.3 copy-start.5
  265.0 4.3 copy-start.6
  270.2 53.7 %copy-start.8 = (bf16[3,64,864]{2,1,0:T(8,128)(2,1)S(1)}, bf16[3,64,864]{2,1,0:T(8,128)(2,1)}, u32[]{:S(2)}) copy-start(bf16[3,64,864]{2,1,0:T(8,128)(2,1)} %param.16) | copy-start | bytes 995332
  315.0 8.9 %copy-start.10 = (f32[512,864]{0,1:T(8,128)S(1)}, f32[512,864]{0,1:T(8,128)}, u32[]{:S(2)}) copy-start(f32[512,864]{0,1:T(8,128)} %copy-done.9) | copy-start | bytes 5308420
  323.9 1.5 copy-start.11
  327.5 7.9 %copy-start.3 = (bf16[3,64,5120]{2,1,0:T(8,128)(2,1)S(1)}, bf16[3,64,5120]{2,1,0:T(8,128)(2,1)}, u32[]{:S(2)}) copy-start(bf16[3,64,5120]{2,1,0:T(8,128)(2,1)} %param.15) | copy-start | bytes 5898244
Sparse Core Ops, SparseCore 0:
  10.3 58.6 all-gather.2
  109.0 117.5 reduce-scatter.3
  261.7 53.2 all-gather.4
  335.5 89.6 all-reduce.3
where the time goes:
time: 438 us
  waiting for transfers between devices  308 us (70%)
  matrix products  53 us (12%)
  blocking collectives  32.2 us (7%)
  local copies, waits for them, and re-layouts  27.5 us (6%)
  between operations  14 us (3%)
    reduce_scatter x1, waiting for transfers between devices, on_device(): lax.psum_scatter(contract_lead(w_down, hidden), 'dp', scatter_dimension=0...  117 us
    psum x1, waiting for transfers between devices, on_device(): out_gate, out_up, in_down = lax.psum((out_gate, out_up, in_down), 'dp')  85 us
    all_gather x1, waiting for transfers between devices, on_device(): piece = lax.all_gather(hidden_in, 'dp', axis=1, tiled=True)  61.1 us
    all_gather x1, waiting for transfers between devices, on_device(): block_cols = lax.all_gather(grad_cols, 'dp', axis=0, tiled=True)  44.8 us
    psum x1, blocking collectives, on_device(): lax.psum((jnp.sum(down_cols * down_cols, axis=0), jnp.sum(scaled * down_c...  32.2 us
    dot_general x3, matrix products, contract_lead(): lax.dot_general(left_mat, right_mat, (((0,), (1,)), ((), ())), preferred_...  22 us
    unnamed x32, local copies, waits for them, and re-layouts  15.9 us
    dot_general x1, matrix products, on_device(): up_value = jnp.dot(piece, w_up, preferred_element_type=jnp.float32)  10.3 us
  transfers between devices with their start and end apart: 4, of which 4 were waited for; matrix products, arithmetic and copies ran while one was open for 3% of the time, Pallas kernels for 0%

commit v1 on v0

--- a/solution.py
+++ b/solution.py
@@ -1,6 +1,10 @@
+import functools
+
 import jax
 import jax.numpy as jnp
 from jax import lax
+from jax.experimental import pallas as pl
+from jax.experimental.pallas import tpu as pltpu
 from jax.sharding import PartitionSpec as P
 
 SEQ = 256
@@ -27,7 +31,7 @@
     return jnp.einsum("stk,stj->skj", inputs_seq, grads_seq, precision=lax.Precision.HIGHEST)
 
 
-def on_device(
+def on_device_plain(
     hidden_in, w_gate, w_up, w_down, norm_gain, out_cotangent, proj_model, proj_hidden, queries
 ):
     width_cols = hidden_in.shape[1]
@@ -88,6 +92,578 @@
     return (block_out, scores)
 
 
+CHUNKS = 2
+BF = jnp.bfloat16
+F32 = jnp.float32
+HIGH = lax.Precision.HIGHEST
+
+
+def matmul(a, b, precision=None):
+    return lax.dot_general(
+        a, b, (((1,), (0,)), ((), ())), precision=precision, preferred_element_type=F32
+    )
+
+
+def matmul_nt(a, b, precision=None):
+    return lax.dot_general(
+        a, b, (((1,), (1,)), ((), ())), precision=precision, preferred_element_type=F32
+    )
+
+
+def fused(
+    n,
+    x_in, cot_in, gain, w_gate, w_up, w_down, proj_model, proj_hidden, queries,
+    out, scores,
+    wg, wu, wd, pm, ph, qs,
+    xa, ga, gate, up, gh, hid, ip_t, od, id_t,
+    xch, xf, cf, ownf, prt, rsr, down, stats, osend, orecv, skp, rsk, skf, pairs,
+    w_sem, m_sem, x_ssem, x_rsem, a_s, a_r, p_s, p_r, b_s, b_r, q_s, q_r,
+    d_s, d_r, r_s, r_r, st_s, st_r, k_s, k_r, f_s, f_r,
+):
+    half = n // 2
+    devices = 2 * n
+    me = lax.axis_index("dp")
+    chip, core = me // 2, lax.rem(me, 2)
+    tokens = x_in.shape[0]
+    narrow = x_in.shape[1]
+    wide = 2 * narrow
+    th = tokens // 2
+    tc = th // CHUNKS
+    width = wide * n
+    seqs = tokens // SEQ
+    rank = od.shape[1]
+    rows_of = 3 * rank
+
+    def chip_at(pos):
+        pos = lax.rem(pos + 2 * n, n)
+        return jnp.where(pos < half, 2 * pos, 2 * (n - 1 - pos) + 1)
+
+    even = lax.rem(chip, 2) == 0
+    here = jnp.where(even, chip // 2, n - 1 - chip // 2)
+    right = chip_at(here + 1) * 2 + core
+    left = chip_at(here - 1) * 2 + core
+    partner = chip * 2 + 1 - core
+    onward = (right, left)
+
+    def cols(q):
+        return pl.ds(pl.multiple_of(q * wide, 128), wide)
+
+    def rows(whose, ch):
+        return pl.ds(pl.multiple_of(whose * th + ch * tc, 16), tc)
+
+    def half_rows(whose):
+        return pl.ds(pl.multiple_of(whose * th, 16), th)
+
+    def remote(src, dst, ssem, rsem, target):
+        return pltpu.make_async_remote_copy(
+            src_ref=src, dst_ref=dst, send_sem=ssem, recv_sem=rsem,
+            device_id={"dp": target}, device_id_type=pl.DeviceIdType.MESH,
+        )
+
+    def weight_copy(which, q):
+        span = pl.ds(pl.multiple_of(q * wide, 16), wide)
+        src, dst = ((w_gate, wg), (w_up, wu))[which]
+        return pltpu.make_async_copy(src.at[span, :], dst.at[span, :], w_sem.at[which, q])
+
+    def block_chip(i):
+        hop = (i + 1) // 2
+        return jnp.where(lax.rem(i, 2) == 1, chip_at(here - hop), chip_at(here + hop))
+
+    pm_copy = pltpu.make_async_copy(proj_model, pm, m_sem.at[0])
+    ph_copy = pltpu.make_async_copy(proj_hidden, ph, m_sem.at[1])
+    wd_copy = pltpu.make_async_copy(w_down, wd, m_sem.at[2])
+    q_copy = pltpu.make_async_copy(queries, qs, m_sem.at[3])
+    for which in range(2):
+        weight_copy(which, chip).start()
+    pm_copy.start()
+
+    @pl.loop(1, n)
+    def _(i):
+        for which in range(2):
+            weight_copy(which, block_chip(i)).start()
+
+    wd_copy.start()
+    ph_copy.start()
+    q_copy.start()
+
+    barrier = pltpu.get_barrier_semaphore()
+
+    @pl.loop(1, devices)
+    def _(o):
+        pl.semaphore_signal(
+            barrier, inc=1, device_id={"dp": lax.rem(me + o, devices)},
+            device_id_type=pl.DeviceIdType.MESH,
+        )
+
+    pl.semaphore_wait(barrier, devices - 1)
+
+    trades = []
+    for at, ref in enumerate((x_in, cot_in)):
+        trades.append(
+            remote(ref.at[half_rows(1 - core), :], xch.at[at], x_ssem.at[at], x_rsem.at[at], partner)
+        )
+        trades[-1].start()
+    for ref in (gate, up, gh, ip_t, od, skp):
+        ref[...] = jnp.zeros_like(ref)
+
+    def join(at, ref, dst):
+        trades[at].wait_recv()
+        mine = ref[half_rows(core), :].astype(F32)
+        theirs = xch[at].astype(F32)
+
+        @pl.when(core == 0)
+        def _():
+            dst[:, :narrow] = mine
+            dst[:, narrow:] = theirs
+
+        @pl.when(core == 1)
+        def _():
+            dst[:, :narrow] = theirs
+            dst[:, narrow:] = mine
+
+    join(0, x_in, xf)
+    xa[half_rows(core), cols(chip)] = xf[...].astype(BF)
+
+    def gather(buf, ssem, rsem, psend, precv, compute, before_loop):
+        def hop(direction, at, ch, q):
+            ref = buf.at[rows(core, ch), cols(q)]
+            where = (direction, at, ch)
+            return remote(ref, ref, ssem.at[where], rsem.at[where], onward[direction])
+
+        def last_hop(direction, ch, q):
+            ref = buf.at[rows(core, ch), cols(q)]
+            return remote(
+                ref, ref, ssem.at[0, half, ch], rsem.at[0, half, ch], onward[direction]
+            )
+
+        def share(direction, at, ch, q, whose):
+            ref = buf.at[rows(whose, ch), cols(q)]
+            where = (direction, at, ch)
+            return remote(ref, ref, psend.at[where], precv.at[where], partner)
+
+        for ch in range(CHUNKS):
+            for direction in range(2):
+                hop(direction, 1, ch, chip).start()
+        for ch in range(CHUNKS):
+            share(0, 0, ch, chip, core).start()
+        before_loop()
+        for ch in range(CHUNKS):
+            share(0, 0, ch, chip, 1 - core).wait_recv()
+        compute(chip)
+
+        @pl.loop(1, n)
+        def _(i):
+            at = (i + 1) // 2
+            odd = lax.rem(i, 2) == 1
+
+            @pl.when(odd & (at < half))
+            def _():
+                for ch in range(CHUNKS):
+                    for direction in range(2):
+                        q = chip_at(here - at) if direction == 0 else chip_at(here + at)
+                        hop(direction, at, ch, q).wait_recv()
+
+                        @pl.when(at < half - 1)
+                        def _():
+                            hop(direction, at + 1, ch, q).start()
+
+                        @pl.when((at == half - 1) & (core == direction))
+                        def _():
+                            last_hop(direction, ch, q).start()
+
+                        share(direction, at, ch, q, core).start()
+
+            @pl.when(i == n - 1)
+            def _():
+                q = chip_at(here - half)
+                for ch in range(CHUNKS):
+                    last_hop(0, ch, q).wait_recv()
+                    share(0, half, ch, q, core).start()
+
+            q = block_chip(i)
+            for ch in range(CHUNKS):
+                share(1 - lax.rem(i, 2), at, ch, q, 1 - core).wait_recv()
+            compute(q)
+
+        def drain():
+            for ch in range(CHUNKS):
+                share(0, 0, ch, chip, core).wait_send()
+                for direction in range(2):
+                    for at in range(1, half):
+                        back = at - 1 if direction == 0 else 1 - at
+                        hop(direction, at, ch, chip_at(here - back)).wait_send()
+                        share(direction, at, ch, chip, core).wait_send()
+                last_hop(0, ch, chip).wait_send()
+                share(0, half, ch, chip, core).wait_send()
+
+        return drain
+
+    def forward(q):
+        for which in range(2):
+            weight_copy(which, q).wait()
+        block = xa[:, cols(q)]
+        span = pl.ds(pl.multiple_of(q * wide, 16), wide)
+        gate[...] += matmul(block, wg[span, :])
+        up[...] += matmul(block, wu[span, :])
+        ip_t[...] += matmul_nt(pm[: 2 * rank, cols(q)], block)
+
+    def first_prep():
+        join(1, cot_in, cf)
+        pm_copy.wait()
+
+    drain = gather(xa, a_s, a_r, p_s, p_r, forward, first_prep)
+
+    piece = 64
+
+    @pl.loop(0, tokens // piece)
+    def _(i):
+        span = pl.ds(pl.multiple_of(i * piece, 16), piece)
+        g = gate[span, :]
+        u = up[span, :]
+        s = jax.nn.sigmoid(g)
+        act = g * s
+        hid[span, :] = (act * u).astype(BF)
+        gate[span, :] = act
+        up[span, :] = u * s * (1.0 + g * (1.0 - s))
+
+    drain()
+    wd_copy.wait()
+
+    def dest(j):
+        far = half - (j + 1) // 2
+        away = jnp.where(lax.rem(j, 2) == 1, far, -far)
+        return jnp.where(
+            j == 0, chip_at(here + half), jnp.where(j == n - 1, chip, chip_at(here + away))
+        )
+
+    def part_copy(j, q):
+        return remote(
+            xa.at[half_rows(1 - core), cols(q)], prt.at[j], d_s.at[j], d_r.at[j], partner
+        )
+
+    def part(j):
+        q = dest(j)
+        xa[half_rows(1 - core), cols(q)] = matmul(
+            hid[half_rows(1 - core), :], wd[:, cols(q)]
+        ).astype(BF)
+        part_copy(j, q).start()
+        ownf[lax.rem(j, 2)] = matmul(hid[half_rows(core), :], wd[:, cols(q)])
+
+    def ring_sum(direction, step, ch, q):
+        return remote(
+            xa.at[rows(core, ch), cols(q)],
+            rsr.at[direction, step, pl.ds(ch * tc, tc), :],
+            r_s.at[direction, step, ch],
+            r_r.at[direction, step, ch],
+            onward[direction],
+        )
+
+    def own_sum(j, ch):
+        span = pl.ds(ch * tc, tc)
+        return ownf[lax.rem(j, 2), span, :] + prt[j, span, :].astype(F32)
+
+    def finish(j):
+        q = dest(j)
+        part_copy(j, q).wait_recv()
+
+        @pl.when(j == 0)
+        def _():
+            for ch in range(CHUNKS):
+                xa[rows(core, ch), cols(q)] = own_sum(j, ch).astype(BF)
+                for direction in range(2):
+
+                    @pl.when(core == direction)
+                    def _():
+                        ring_sum(direction, 0, ch, q).start()
+
+        step = (j + 1) // 2
+        for direction in range(2):
+
+            @pl.when((j > 0) & (lax.rem(j, 2) == 1 - direction))
+            def _():
+                for ch in range(CHUNKS):
+                    span = pl.ds(ch * tc, tc)
+                    carried = (step > 1) | (core == direction)
+
+                    @pl.when(carried)
+                    def _():
+                        ring_sum(direction, step - 1, ch, q).wait_recv()
+                        xa[rows(core, ch), cols(q)] = (
+                            own_sum(j, ch) + rsr[direction, step - 1, span, :].astype(F32)
+                        ).astype(BF)
+
+                    @pl.when(jnp.logical_not(carried))
+                    def _():
+                        xa[rows(core, ch), cols(q)] = own_sum(j, ch).astype(BF)
+
+                    ring_sum(direction, step, ch, q).start()
+
+    part(0)
+
+    @pl.loop(1, n)
+    def _(j):
+        part(j)
+        finish(j - 1)
+
+    part_copy(n - 1, chip).wait_recv()
+    for ch in range(CHUNKS):
+        span = pl.ds(ch * tc, tc)
+        for direction in range(2):
+            ring_sum(direction, half - 1, ch, chip).wait_recv()
+        down[span, :] = (
+            own_sum(n - 1, ch)
+            + rsr[0, half - 1, span, :].astype(F32)
+            + rsr[1, half - 1, span, :].astype(F32)
+        )
+
+    gains = gain[:, cols(chip)]
+    ones = jnp.ones((8, 128), F32)
+
+    def fold(v):
+        total = v[:, :128]
+        for at in range(128, wide, 128):
+            total = total + v[:, at : at + 128]
+        return matmul_nt(ones, total, HIGH)
+
+    stats[chip, 0:8, :] = fold(down[...] * down[...])
+    stats[chip, 8:16, :] = fold(gains * cf[...] * down[...])
+
+    def stat_copy(o):
+        other = lax.rem(chip + o, n)
+        ref = stats.at[chip]
+        return remote(ref, ref, st_s.at[o], st_r.at[o], other * 2 + core)
+
+    def stat_recv(o):
+        ref = stats.at[lax.rem(chip + n - o, n)]
+        return remote(ref, ref, st_s.at[o], st_r.at[o], partner)
+
+    for o in range(1, n):
+        stat_copy(o).start()
+    for o in range(1, n):
+        stat_recv(o).wait_recv()
+    total = stats[0]
+    for at in range(1, n):
+        total = total + stats[at]
+    inv_row = lax.rsqrt(total[0:8] / width + epsilon)
+    mean_row = total[8:16] / width
+    turned = jnp.transpose(jnp.concatenate([inv_row] * 8 + [mean_row] * 8, axis=0))
+    inv_rms = turned[:, 0:1]
+    mixed_mean = turned[:, 64:65]
+    normed = down[...] * inv_rms
+    ga[half_rows(core), cols(chip)] = (
+        inv_rms * (gains * cf[...] - normed * (inv_rms * mixed_mean))
+    ).astype(BF)
+    xf[...] = xf[...] + normed * gains
+
+    out_copy = remote(osend, orecv, m_sem.at[4], m_sem.at[5], partner)
+
+    def block_output():
+        @pl.when(core == 0)
+        def _():
+            osend[...] = xf[:, narrow:].astype(BF)
+            out[half_rows(0), :] = xf[:, :narrow].astype(BF)
+
+        @pl.when(core == 1)
+        def _():
+            osend[...] = xf[:, :narrow].astype(BF)
+            out[half_rows(1), :] = xf[:, narrow:].astype(BF)
+
+        out_copy.start()
+        ph_copy.wait()
+        id_t[...] = matmul_nt(ph[2 * rank :, :], hid[...])
+
+    def backward(q):
+        block = ga[:, cols(q)]
+        gh[...] += matmul_nt(block, wd[:, cols(q)])
+        od[...] += matmul_nt(block, pm[2 * rank :, cols(q)])
+
+    drain = gather(ga, b_s, b_r, q_s, q_r, backward, block_output)
+
+    for s in range(seqs):
+        span = pl.ds(s * SEQ, SEQ)
+        lanes = slice(s * SEQ, (s + 1) * SEQ)
+        back = gh[span, :]
+        out_gate = matmul_nt((back * up[span, :]).astype(BF), ph[:rank, :])
+        out_up = matmul_nt((back * gate[span, :]).astype(BF), ph[rank : 2 * rank, :])
+        first = s * rows_of
+        skp[first : first + rank, :rank] = matmul(ip_t[:rank, lanes], out_gate, HIGH)
+        skp[first + rank : first + 2 * rank, :rank] = matmul(ip_t[rank:, lanes], out_up, HIGH)
+        skp[first + 2 * rank : first + 3 * rank, :rank] = matmul(
+            id_t[:, lanes], od[span, :], HIGH
+        )
+
+    share = seqs * rows_of // devices
+
+    def share_rows(d):
+        return pl.ds(pl.multiple_of(d * share, 8), share)
+
+    def scatter(o):
+        to = lax.rem(me + o, devices)
+        return remote(skp.at[share_rows(to), :], rsk.at[o], k_s.at[o], k_r.at[o], to)
+
+    @pl.loop(1, devices)
+    def _(o):
+        scatter(o).start()
+
+    rsk[0] = skp[share_rows(me), :]
+
+    @pl.loop(1, devices)
+    def _(o):
+        scatter(o).wait_recv()
+
+    summed = rsk[0]
+    for o in range(1, devices):
+        summed = summed + rsk[o]
+    skf[share_rows(me), :] = summed
+
+    def spread(o):
+        ref = skf.at[share_rows(me), :]
+        return remote(ref, ref, f_s.at[o], f_r.at[o], lax.rem(me + o, devices))
+
+    def spread_recv(o):
+        ref = skf.at[share_rows(lax.rem(me + devices - o, devices)), :]
+        return remote(ref, ref, f_s.at[o], f_r.at[o], partner)
+
+    @pl.loop(1, devices)
+    def _(o):
+        spread(o).start()
+
+    out_copy.wait_recv()
+    for k in range(2):
+
+        @pl.when(core == k)
+        def _():
+            out[half_rows(1 - k), :] = orecv[...]
+
+    drain()
+    out_copy.wait_send()
+    for trade in trades:
+        trade.wait_send()
+    for j in range(n):
+        part_copy(j, chip).wait_send()
+    for ch in range(CHUNKS):
+        for direction in range(2):
+            for step in range(1, half):
+                ring_sum(direction, step, ch, chip).wait_send()
+
+            @pl.when(core == direction)
+            def _():
+                ring_sum(direction, 0, ch, chip).wait_send()
+
+    for o in range(1, n):
+        stat_copy(o).wait_send()
+
+    @pl.loop(1, devices)
+    def _(o):
+        scatter(o).wait_send()
+
+    q_copy.wait()
+
+    @pl.loop(1, devices)
+    def _(o):
+        spread_recv(o).wait_recv()
+
+    count = seqs * rows_of // 2
+    pairs[:, :rank] = skf[pl.ds(0, count, stride=2), :][:, :rank]
+    pairs[:, rank:] = skf[pl.ds(1, count, stride=2), :][:, :rank]
+    tiles = rows_of // 2
+
+    def add(t, sums):
+        tile = qs[:, pl.ds(pl.multiple_of(t * 2 * rank, 128), 2 * rank)].astype(F32)
+        return tuple(
+            sums[s] + tile * pairs[pl.ds(s * tiles + t, 1), :] for s in range(seqs)
+        )
+
+    zero = jnp.zeros((qs.shape[0], 2 * rank), F32)
+    sums = lax.fori_loop(0, tiles, add, (zero,) * seqs)
+    for s in range(seqs):
+        scores[s : s + 1, :] = matmul_nt(ones, sums[s], HIGH)[0:1, :]
+
+    @pl.loop(1, devices)
+    def _(o):
+        spread(o).wait_send()
+
+
+def fused_fits(hidden_in, proj_model, queries, devices):
+    n = devices // 2
+    tokens, narrow = hidden_in.shape
+    rank = proj_model.shape[1]
+    rows_of = tokens // SEQ * 3 * rank
+    return (
+        devices % 4 == 0
+        and n >= 4
+        and (2 * narrow) % 128 == 0
+        and rank == 64
+        and tokens % (SEQ * 2) == 0
+        and rows_of % (8 * devices) == 0
+    )
+
+
+def on_device_fused(
+    hidden_in, w_gate, w_up, w_down, norm_gain, out_cotangent, proj_model, proj_hidden, queries
+):
+    devices = lax.axis_size("dp")
+    n = devices // 2
+    half = n // 2
+    tokens, narrow = hidden_in.shape
+    wide, th = 2 * narrow, tokens // 2
+    width, units = w_gate.shape
+    rank = proj_model.shape[1]
+    seqs = tokens // SEQ
+    sk_rows = seqs * 3 * rank
+    vmem = pltpu.VMEM
+    dma = pltpu.SemaphoreType.DMA
+    block = (th, wide)
+    scratch = [
+        vmem((width, units), BF), vmem((width, units), BF), vmem((units, width), BF),
+        vmem((3 * rank, width), BF), vmem((3 * rank, units), BF), vmem(queries.shape, BF),
+        vmem((tokens, width), BF), vmem((tokens, width), BF),
+        vmem((tokens, units), F32), vmem((tokens, units), F32), vmem((tokens, units), F32),
+        vmem((tokens, units), BF), vmem((2 * rank, tokens), F32), vmem((tokens, rank), F32),
+        vmem((rank, tokens), F32),
+        vmem((2, th, narrow), BF), vmem(block, F32), vmem(block, F32),
+        vmem((2,) + block, F32), vmem((n,) + block, BF), vmem((2, half) + block, BF),
+        vmem(block, F32), vmem((n, 16, th), F32),
+        vmem((th, narrow), BF), vmem((th, narrow), BF),
+        vmem((sk_rows, 128), F32), vmem((devices, sk_rows // devices, 128), F32),
+        vmem((sk_rows, 128), F32), vmem((sk_rows // 2, 2 * rank), F32),
+        dma((2, n)), dma((6,)), dma((2,)), dma((2,)),
+    ]
+    scratch += [dma((2, half + 1, CHUNKS))] * 8
+    scratch += [dma((n,))] * 2 + [dma((2, half, CHUNKS))] * 2 + [dma((n,))] * 2
+    scratch += [dma((devices,))] * 4
+    near = pl.BlockSpec(memory_space=pltpu.VMEM)
+    far = pl.BlockSpec(memory_space=pl.ANY)
+    return pl.pallas_call(
+        functools.partial(fused, n),
+        out_shape=(
+            jax.ShapeDtypeStruct((tokens, narrow), BF),
+            jax.ShapeDtypeStruct((seqs, queries.shape[0]), F32),
+        ),
+        in_specs=[near, near, near] + [far] * 6,
+        out_specs=(near, near),
+        scratch_shapes=scratch,
+        compiler_params=pltpu.CompilerParams(
+            collective_id=0, has_side_effects=True, vmem_limit_bytes=VMEM_LIMIT
+        ),
+    )(
+        hidden_in, out_cotangent, norm_gain[None, :], w_gate, w_up, w_down,
+        proj_model.reshape(3 * rank, width), proj_hidden.reshape(3 * rank, units), queries,
+    )
+
+
+VMEM_LIMIT = 63 * 1024 * 1024
+
+
+def on_device(hidden_in, w_gate, w_up, w_down, norm_gain, out_cotangent, proj_model, *rest):
+    form = on_device_plain
+    if fused_fits(hidden_in, proj_model, rest[1], lax.axis_size("dp")):
+        form = on_device_fused
+    return form(
+        hidden_in, w_gate, w_up, w_down, norm_gain, out_cotangent, proj_model, *rest
+    )
+
+
 def solution(mesh):
     in_specs = (
         P("group", "dp"),

time: 438 us -> 158 us (0.36)
  waiting for transfers between devices: 308 us -> 0 us
  Pallas kernels: 0 us -> 124 us
  matrix products: 53 us -> 0 us
  blocking collectives: 32.2 us -> 0 us
  between operations: 14 us -> 0.64 us
  local copies, waits for them, and re-layouts: 27.5 us -> 32.3 us
    pallas_call x0 -> x1, Pallas kernels: none -> 124 us  [on_device_fused(): pl.pallas_call(functools.partial(fused, n), out_shape=(jax.ShapeDtypeStru...]
    reduce_scatter x1 -> x0, waiting for transfers between devices: 117 us -> none  [on_device(): lax.psum_scatter(contract_lead(w_down, hidden), 'dp', scatter_dimension=0...]
    all_gather x2 -> x0, waiting for transfers between devices: 106 us -> none  [the longest x1 61.1 us: on_device(): piece = lax.all_gather(hidden_in, 'dp', axis=1, tiled=True)]
    psum x1 -> x0, waiting for transfers between devices: 85 us -> none  [on_device(): out_gate, out_up, in_down = lax.psum((out_gate, out_up, in_down), 'dp')]
    dot_general x13 -> x0, matrix products: 53 us -> none  [the longest x3 22 us: contract_lead(): lax.dot_general(left_mat, right_mat, (((0,), (1,)), ((), ())), preferred_...]
    psum x1 -> x0, blocking collectives: 32.2 us -> none  [on_device(): lax.psum((jnp.sum(down_cols * down_cols, axis=0), jnp.sum(scaled * down_c...]
    unnamed x32 -> x5, local copies, waits for them, and re-layouts: 15.9 us -> 30.5 us
    dot_general x1 -> x0, local copies, waits for them, and re-layouts: 7.91 us -> none  [contract_lead(): lax.dot_general(left_mat, right_mat, (((0,), (1,)), ((), ())), preferred_...]
  transfers between devices with their start and end apart: 4 -> 0, of which waited for: 4 -> 0; matrix products, arithmetic and copies ran while one was open for 3% -> 0% of each run, Pallas kernels for 0% -> 0%
where the time goes in v1:
time: 158 us; the launch traced here: 157 us
  Pallas kernels  124 us (78%)
  local copies, waits for them, and re-layouts  32.3 us (20%)
    pallas_call x1, Pallas kernels, on_device_fused(): pl.pallas_call(functools.partial(fused, n), out_shape=(jax.ShapeDtypeStru...  124 us
    unnamed x5, local copies, waits for them, and re-layouts  30.5 us

profile of v1, /device:TPU:0, one launch (start us, length us, event | category | flops | bytes accessed | tf_op | source)
XLA Modules:
  0.0 157.2 jit_solution(9723488867834078244)
XLA Ops:
  0.6 1.9 %copy.11.x_in = bf16[512,320]{1,0:T(8,128)(2,1)} copy(bf16[512,320]{0,1:T(8,128)(2,1)} %param.9) | data formatting | bytes 655360 | tf_op args[0]
  2.5 1.9 %copy.12.cot_in = bf16[512,320]{1,0:T(8,128)(2,1)} copy(bf16[512,320]{0,1:T(8,128)(2,1)} %param.14) | data formatting | bytes 655360 | tf_op args[5]
  4.4 12.7 %copy.13.w_gate = bf16[5120,864]{1,0:T(8,128)(2,1)} copy(bf16[5120,864]{0,1:T(8,128)(2,1)} %param.10) | data formatting | bytes 17694720 | tf_op args[1]
  17.1 12.7 %copy.14.w_up = bf16[5120,864]{1,0:T(8,128)(2,1)} copy(bf16[5120,864]{0,1:T(8,128)(2,1)} %param.11) | data formatting | bytes 17694720 | tf_op args[2]
  29.9 124.2 %shard_map.104 = (bf16[512,320]{1,0:T(8,128)(2,1)}, f32[2,64]{1,0:T(2,128)}) custom-call(bf16[512,320]{1,0:T(8,128)(2,1)} %copy.11.x_in, bf16[512,320]{1,0:T(8,128)(2,1)} %copy.12.cot_in, f32[1,5120]{1,0:T(1,128)} %bitcast.5, bf16[5120,864]{1,0:T(8,128)(2,1)} %copy.13.w_gate, bf16[5120,864]{1,0:T(8,128)(2,1)} %copy.14.w_up, bf16[864,5120]{1,0:T(8,128)(2,1)} %w_down.1, ...), custom_call_target="tpu_custom_call" | custom-call | tf_op jit(solution)/shard_map/pallas_call | solution.py:637
  154.1 1.9 %copy.15 = bf16[512,320]{0,1:T(8,128)(2,1)} copy(bf16[512,320]{1,0:T(8,128)(2,1)} %get-tuple-element.2) | data formatting | bytes 655360 | tf_op jit(solution)/shard_map/pallas_call | solution.py:637
  156.0 1.2 copy.17

commit v2 on v1

--- a/solution.py
+++ b/solution.py
@@ -110,13 +110,17 @@
     )
 
 
+def matmul_tn(a, b):
+    return lax.dot_general(a, b, (((0,), (0,)), ((), ())), preferred_element_type=F32)
+
+
 def fused(
     n,
     x_in, cot_in, gain, w_gate, w_up, w_down, proj_model, proj_hidden, queries,
     out, scores,
     wg, wu, wd, pm, ph, qs,
-    xa, ga, gate, up, gh, hid, ip_t, od, id_t,
-    xch, xf, cf, ownf, prt, rsr, down, stats, osend, orecv, skp, rsk, skf, pairs,
+    xa, ga, gate, up, gh, hid, ip_t, od_t, id_t,
+    xch, xf, cf, gcol, ownf, prt, rsr, down, stats, osend, orecv, skp, rsk, skf, pairs,
     w_sem, m_sem, x_ssem, x_rsem, a_s, a_r, p_s, p_r, b_s, b_r, q_s, q_r,
     d_s, d_r, r_s, r_r, st_s, st_r, k_s, k_r, f_s, f_r,
 ):
@@ -124,14 +128,13 @@
     devices = 2 * n
     me = lax.axis_index("dp")
     chip, core = me // 2, lax.rem(me, 2)
-    tokens = x_in.shape[0]
-    narrow = x_in.shape[1]
+    narrow, tokens = x_in.shape
     wide = 2 * narrow
     th = tokens // 2
-    tc = th // CHUNKS
+    fc = wide // CHUNKS
     width = wide * n
     seqs = tokens // SEQ
-    rank = od.shape[1]
+    rank = od_t.shape[0]
     rows_of = 3 * rank
 
     def chip_at(pos):
@@ -148,11 +151,14 @@
     def cols(q):
         return pl.ds(pl.multiple_of(q * wide, 128), wide)
 
-    def rows(whose, ch):
-        return pl.ds(pl.multiple_of(whose * th + ch * tc, 16), tc)
-
-    def half_rows(whose):
-        return pl.ds(pl.multiple_of(whose * th, 16), th)
+    def feats(q, ch):
+        return pl.ds(pl.multiple_of(q * wide + ch * fc, 16), fc)
+
+    def all_feats(q):
+        return pl.ds(pl.multiple_of(q * wide, 16), wide)
+
+    def lanes(whose):
+        return pl.ds(pl.multiple_of(whose * th, 128), th)
 
     def remote(src, dst, ssem, rsem, target):
         return pltpu.make_async_remote_copy(
@@ -161,9 +167,8 @@
         )
 
     def weight_copy(which, q):
-        span = pl.ds(pl.multiple_of(q * wide, 16), wide)
         src, dst = ((w_gate, wg), (w_up, wu))[which]
-        return pltpu.make_async_copy(src.at[span, :], dst.at[span, :], w_sem.at[which, q])
+        return pltpu.make_async_copy(src.at[:, cols(q)], dst.at[:, cols(q)], w_sem.at[which, q])
 
     def block_chip(i):
         hop = (i + 1) // 2
@@ -200,44 +205,36 @@
     trades = []
     for at, ref in enumerate((x_in, cot_in)):
         trades.append(
-            remote(ref.at[half_rows(1 - core), :], xch.at[at], x_ssem.at[at], x_rsem.at[at], partner)
+            remote(ref.at[:, lanes(1 - core)], xch.at[at], x_ssem.at[at], x_rsem.at[at], partner)
         )
         trades[-1].start()
-    for ref in (gate, up, gh, ip_t, od, skp):
+    for ref in (gate, up, gh, ip_t, od_t, skp):
         ref[...] = jnp.zeros_like(ref)
 
     def join(at, ref, dst):
         trades[at].wait_recv()
-        mine = ref[half_rows(core), :].astype(F32)
-        theirs = xch[at].astype(F32)
-
-        @pl.when(core == 0)
-        def _():
-            dst[:, :narrow] = mine
-            dst[:, narrow:] = theirs
-
-        @pl.when(core == 1)
-        def _():
-            dst[:, :narrow] = theirs
-            dst[:, narrow:] = mine
-
+        dst[own_feats, :] = ref[:, lanes(core)].astype(F32)
+        dst[other_feats, :] = xch[at].astype(F32)
+
+    own_feats = pl.ds(pl.multiple_of(core * narrow, 16), narrow)
+    other_feats = pl.ds(pl.multiple_of((1 - core) * narrow, 16), narrow)
     join(0, x_in, xf)
-    xa[half_rows(core), cols(chip)] = xf[...].astype(BF)
+    xa[all_feats(chip), lanes(core)] = xf[...].astype(BF)
 
     def gather(buf, ssem, rsem, psend, precv, compute, before_loop):
         def hop(direction, at, ch, q):
-            ref = buf.at[rows(core, ch), cols(q)]
+            ref = buf.at[feats(q, ch), lanes(core)]
             where = (direction, at, ch)
             return remote(ref, ref, ssem.at[where], rsem.at[where], onward[direction])
 
         def last_hop(direction, ch, q):
-            ref = buf.at[rows(core, ch), cols(q)]
+            ref = buf.at[feats(q, ch), lanes(core)]
             return remote(
                 ref, ref, ssem.at[0, half, ch], rsem.at[0, half, ch], onward[direction]
             )
 
         def share(direction, at, ch, q, whose):
-            ref = buf.at[rows(whose, ch), cols(q)]
+            ref = buf.at[feats(q, ch), lanes(whose)]
             where = (direction, at, ch)
             return remote(ref, ref, psend.at[where], precv.at[where], partner)
 
@@ -301,21 +298,22 @@
     def forward(q):
         for which in range(2):
             weight_copy(which, q).wait()
-        block = xa[:, cols(q)]
-        span = pl.ds(pl.multiple_of(q * wide, 16), wide)
-        gate[...] += matmul(block, wg[span, :])
-        up[...] += matmul(block, wu[span, :])
-        ip_t[...] += matmul_nt(pm[: 2 * rank, cols(q)], block)
+        block = xa[all_feats(q), :]
+        gate[...] += matmul(wg[:, cols(q)], block)
+        up[...] += matmul(wu[:, cols(q)], block)
+        ip_t[...] += matmul(pm[: 2 * rank, cols(q)], block)
 
     def first_prep():
         join(1, cot_in, cf)
+        gcol[...] = jnp.transpose(jnp.broadcast_to(gain[:, cols(chip)], (128, wide)))
+        cf[...] = gcol[:, 0:1] * cf[...]
         pm_copy.wait()
 
     drain = gather(xa, a_s, a_r, p_s, p_r, forward, first_prep)
 
-    piece = 64
-
-    @pl.loop(0, tokens // piece)
+    piece = 32
+
+    @pl.loop(0, gate.shape[0] // piece)
     def _(i):
         span = pl.ds(pl.multiple_of(i * piece, 16), piece)
         g = gate[span, :]
@@ -338,29 +336,28 @@
 
     def part_copy(j, q):
         return remote(
-            xa.at[half_rows(1 - core), cols(q)], prt.at[j], d_s.at[j], d_r.at[j], partner
+            xa.at[all_feats(q), lanes(1 - core)], prt.at[j], d_s.at[j], d_r.at[j], partner
         )
 
     def part(j):
         q = dest(j)
-        xa[half_rows(1 - core), cols(q)] = matmul(
-            hid[half_rows(1 - core), :], wd[:, cols(q)]
-        ).astype(BF)
+        slot = lax.rem(j, 2)
+        ownf[slot] = matmul_tn(wd[:, cols(q)], hid[...])
+        xa[all_feats(q), lanes(1 - core)] = ownf[slot, :, lanes(1 - core)].astype(BF)
         part_copy(j, q).start()
-        ownf[lax.rem(j, 2)] = matmul(hid[half_rows(core), :], wd[:, cols(q)])
 
     def ring_sum(direction, step, ch, q):
         return remote(
-            xa.at[rows(core, ch), cols(q)],
-            rsr.at[direction, step, pl.ds(ch * tc, tc), :],
+            xa.at[feats(q, ch), lanes(core)],
+            rsr.at[direction, step, pl.ds(ch * fc, fc), :],
             r_s.at[direction, step, ch],
             r_r.at[direction, step, ch],
             onward[direction],
         )
 
     def own_sum(j, ch):
-        span = pl.ds(ch * tc, tc)
-        return ownf[lax.rem(j, 2), span, :] + prt[j, span, :].astype(F32)
+        span = pl.ds(ch * fc, fc)
+        return ownf[lax.rem(j, 2), span, lanes(core)] + prt[j, span, :].astype(F32)
 
     def finish(j):
         q = dest(j)
@@ -369,7 +366,7 @@
         @pl.when(j == 0)
         def _():
             for ch in range(CHUNKS):
-                xa[rows(core, ch), cols(q)] = own_sum(j, ch).astype(BF)
+                xa[feats(q, ch), lanes(core)] = own_sum(j, ch).astype(BF)
                 for direction in range(2):
 
                     @pl.when(core == direction)
@@ -382,19 +379,19 @@
             @pl.when((j > 0) & (lax.rem(j, 2) == 1 - direction))
             def _():
                 for ch in range(CHUNKS):
-                    span = pl.ds(ch * tc, tc)
+                    span = pl.ds(ch * fc, fc)
                     carried = (step > 1) | (core == direction)
 
                     @pl.when(carried)
                     def _():
                         ring_sum(direction, step - 1, ch, q).wait_recv()
-                        xa[rows(core, ch), cols(q)] = (
+                        xa[feats(q, ch), lanes(core)] = (
                             own_sum(j, ch) + rsr[direction, step - 1, span, :].astype(F32)
                         ).astype(BF)
 
                     @pl.when(jnp.logical_not(carried))
                     def _():
-                        xa[rows(core, ch), cols(q)] = own_sum(j, ch).astype(BF)
+                        xa[feats(q, ch), lanes(core)] = own_sum(j, ch).astype(BF)
 
                     ring_sum(direction, step, ch, q).start()
 
@@ -407,7 +404,7 @@
 
     part_copy(n - 1, chip).wait_recv()
     for ch in range(CHUNKS):
-        span = pl.ds(ch * tc, tc)
+        span = pl.ds(ch * fc, fc)
         for direction in range(2):
             ring_sum(direction, half - 1, ch, chip).wait_recv()
         down[span, :] = (
@@ -416,17 +413,12 @@
             + rsr[1, half - 1, span, :].astype(F32)
         )
 
-    gains = gain[:, cols(chip)]
-    ones = jnp.ones((8, 128), F32)
-
     def fold(v):
-        total = v[:, :128]
-        for at in range(128, wide, 128):
-            total = total + v[:, at : at + 128]
-        return matmul_nt(ones, total, HIGH)
-
-    stats[chip, 0:8, :] = fold(down[...] * down[...])
-    stats[chip, 8:16, :] = fold(gains * cf[...] * down[...])
+        return jnp.sum(v, axis=0, keepdims=True)
+
+    stats[chip] = jnp.concatenate(
+        [fold(down[...] * down[...]), fold(cf[...] * down[...]), jnp.zeros((6, th), F32)], axis=0
+    )
 
     def stat_copy(o):
         other = lax.rem(chip + o, n)
@@ -444,52 +436,41 @@
     total = stats[0]
     for at in range(1, n):
         total = total + stats[at]
-    inv_row = lax.rsqrt(total[0:8] / width + epsilon)
-    mean_row = total[8:16] / width
-    turned = jnp.transpose(jnp.concatenate([inv_row] * 8 + [mean_row] * 8, axis=0))
-    inv_rms = turned[:, 0:1]
-    mixed_mean = turned[:, 64:65]
+    inv_rms = lax.rsqrt(total[0:1] / width + epsilon)
+    mixed_mean = total[1:2] / width
     normed = down[...] * inv_rms
-    ga[half_rows(core), cols(chip)] = (
-        inv_rms * (gains * cf[...] - normed * (inv_rms * mixed_mean))
+    ga[all_feats(chip), lanes(core)] = (
+        inv_rms * (cf[...] - normed * (inv_rms * mixed_mean))
     ).astype(BF)
-    xf[...] = xf[...] + normed * gains
 
     out_copy = remote(osend, orecv, m_sem.at[4], m_sem.at[5], partner)
 
     def block_output():
-        @pl.when(core == 0)
-        def _():
-            osend[...] = xf[:, narrow:].astype(BF)
-            out[half_rows(0), :] = xf[:, :narrow].astype(BF)
-
-        @pl.when(core == 1)
-        def _():
-            osend[...] = xf[:, :narrow].astype(BF)
-            out[half_rows(1), :] = xf[:, narrow:].astype(BF)
-
+        xf[...] = xf[...] + down[...] * inv_rms * gcol[:, 0:1]
+        osend[...] = xf[other_feats, :].astype(BF)
         out_copy.start()
+        out[:, lanes(core)] = xf[own_feats, :].astype(BF)
         ph_copy.wait()
-        id_t[...] = matmul_nt(ph[2 * rank :, :], hid[...])
+        id_t[...] = matmul(ph[2 * rank :, :], hid[...])
 
     def backward(q):
-        block = ga[:, cols(q)]
-        gh[...] += matmul_nt(block, wd[:, cols(q)])
-        od[...] += matmul_nt(block, pm[2 * rank :, cols(q)])
+        block = ga[all_feats(q), :]
+        gh[...] += matmul(wd[:, cols(q)], block)
+        od_t[...] += matmul(pm[2 * rank :, cols(q)], block)
 
     drain = gather(ga, b_s, b_r, q_s, q_r, backward, block_output)
 
+    out_gate = matmul(ph[:rank, :], (gh[...] * up[...]).astype(BF))
+    out_up = matmul(ph[rank : 2 * rank, :], (gh[...] * gate[...]).astype(BF))
     for s in range(seqs):
-        span = pl.ds(s * SEQ, SEQ)
-        lanes = slice(s * SEQ, (s + 1) * SEQ)
-        back = gh[span, :]
-        out_gate = matmul_nt((back * up[span, :]).astype(BF), ph[:rank, :])
-        out_up = matmul_nt((back * gate[span, :]).astype(BF), ph[rank : 2 * rank, :])
+        at = slice(s * SEQ, (s + 1) * SEQ)
         first = s * rows_of
-        skp[first : first + rank, :rank] = matmul(ip_t[:rank, lanes], out_gate, HIGH)
-        skp[first + rank : first + 2 * rank, :rank] = matmul(ip_t[rank:, lanes], out_up, HIGH)
-        skp[first + 2 * rank : first + 3 * rank, :rank] = matmul(
-            id_t[:, lanes], od[span, :], HIGH
+        skp[first : first + rank, :rank] = matmul_nt(ip_t[:rank, at], out_gate[:, at], HIGH)
+        skp[first + rank : first + 2 * rank, :rank] = matmul_nt(
+            ip_t[rank:, at], out_up[:, at], HIGH
+        )
+        skp[first + 2 * rank : first + 3 * rank, :rank] = matmul_nt(
+            id_t[:, at], od_t[:, at], HIGH
         )
 
     share = seqs * rows_of // devices
@@ -529,11 +510,7 @@
         spread(o).start()
 
     out_copy.wait_recv()
-    for k in range(2):
-
-        @pl.when(core == k)
-        def _():
-            out[half_rows(1 - k), :] = orecv[...]
+    out[:, lanes(1 - core)] = orecv[...]
 
     drain()
     out_copy.wait_send()
@@ -576,6 +553,7 @@
 
     zero = jnp.zeros((qs.shape[0], 2 * rank), F32)
     sums = lax.fori_loop(0, tiles, add, (zero,) * seqs)
+    ones = jnp.ones((8, 2 * rank), F32)
     for s in range(seqs):
         scores[s : s + 1, :] = matmul_nt(ones, sums[s], HIGH)[0:1, :]
 
@@ -584,7 +562,7 @@
         spread(o).wait_send()
 
 
-def fused_fits(hidden_in, proj_model, queries, devices):
+def fused_fits(hidden_in, w_down, proj_model, devices):
     n = devices // 2
     tokens, narrow = hidden_in.shape
     rank = proj_model.shape[1]
@@ -595,6 +573,9 @@
         and (2 * narrow) % 128 == 0
         and rank == 64
         and tokens % (SEQ * 2) == 0
+        and (2 * narrow) % (16 * CHUNKS) == 0
+        and narrow % 16 == 0
+        and w_down.shape[0] % 32 == 0
         and rows_of % (8 * devices) == 0
     )
 
@@ -613,18 +594,18 @@
     sk_rows = seqs * 3 * rank
     vmem = pltpu.VMEM
     dma = pltpu.SemaphoreType.DMA
-    block = (th, wide)
+    block = (wide, th)
     scratch = [
-        vmem((width, units), BF), vmem((width, units), BF), vmem((units, width), BF),
+        vmem((units, width), BF), vmem((units, width), BF), vmem((units, width), BF),
         vmem((3 * rank, width), BF), vmem((3 * rank, units), BF), vmem(queries.shape, BF),
-        vmem((tokens, width), BF), vmem((tokens, width), BF),
-        vmem((tokens, units), F32), vmem((tokens, units), F32), vmem((tokens, units), F32),
-        vmem((tokens, units), BF), vmem((2 * rank, tokens), F32), vmem((tokens, rank), F32),
+        vmem((width, tokens), BF), vmem((width, tokens), BF),
+        vmem((units, tokens), F32), vmem((units, tokens), F32), vmem((units, tokens), F32),
+        vmem((units, tokens), BF), vmem((2 * rank, tokens), F32), vmem((rank, tokens), F32),
         vmem((rank, tokens), F32),
-        vmem((2, th, narrow), BF), vmem(block, F32), vmem(block, F32),
-        vmem((2,) + block, F32), vmem((n,) + block, BF), vmem((2, half) + block, BF),
-        vmem(block, F32), vmem((n, 16, th), F32),
-        vmem((th, narrow), BF), vmem((th, narrow), BF),
+        vmem((2, narrow, th), BF), vmem(block, F32), vmem(block, F32), vmem((wide, 128), F32),
+        vmem((2, wide, tokens), F32), vmem((n,) + block, BF), vmem((2, half) + block, BF),
+        vmem(block, F32), vmem((n, 8, th), F32),
+        vmem((narrow, th), BF), vmem((narrow, th), BF),
         vmem((sk_rows, 128), F32), vmem((devices, sk_rows // devices, 128), F32),
         vmem((sk_rows, 128), F32), vmem((sk_rows // 2, 2 * rank), F32),
         dma((2, n)), dma((6,)), dma((2,)), dma((2,)),
@@ -634,10 +615,10 @@
     scratch += [dma((devices,))] * 4
     near = pl.BlockSpec(memory_space=pltpu.VMEM)
     far = pl.BlockSpec(memory_space=pl.ANY)
-    return pl.pallas_call(
+    block_out, scores = pl.pallas_call(
         functools.partial(fused, n),
         out_shape=(
-            jax.ShapeDtypeStruct((tokens, narrow), BF),
+            jax.ShapeDtypeStruct((narrow, tokens), BF),
             jax.ShapeDtypeStruct((seqs, queries.shape[0]), F32),
         ),
         in_specs=[near, near, near] + [far] * 6,
@@ -647,9 +628,10 @@
             collective_id=0, has_side_effects=True, vmem_limit_bytes=VMEM_LIMIT
         ),
     )(
-        hidden_in, out_cotangent, norm_gain[None, :], w_gate, w_up, w_down,
+        hidden_in.T, out_cotangent.T, norm_gain[None, :], w_gate.T, w_up.T, w_down,
         proj_model.reshape(3 * rank, width), proj_hidden.reshape(3 * rank, units), queries,
     )
+    return block_out.T, scores
 
 
 VMEM_LIMIT = 63 * 1024 * 1024
@@ -657,7 +639,7 @@
 
 def on_device(hidden_in, w_gate, w_up, w_down, norm_gain, out_cotangent, proj_model, *rest):
     form = on_device_plain
-    if fused_fits(hidden_in, proj_model, rest[1], lax.axis_size("dp")):
+    if fused_fits(hidden_in, w_down, proj_model, lax.axis_size("dp")):
         form = on_device_fused
     return form(
         hidden_in, w_gate, w_up, w_down, norm_gain, out_cotangent, proj_model, *rest

time: 158 us -> 126 us (0.80)
  local copies, waits for them, and re-layouts: 32.3 us -> 2.96 us
  Pallas kernels: 124 us -> 122 us
    unnamed x5 -> x2, local copies, waits for them, and re-layouts: 30.5 us -> 2.96 us
    pallas_call x1, Pallas kernels: 124 us -> 122 us  [on_device_fused(): pl.pallas_call(functools.partial(fused, n), out_shape=(jax.ShapeDtypeStru...]
    pallas_call x1 -> x0, local copies, waits for them, and re-layouts: 1.88 us -> none  [on_device_fused(): pl.pallas_call(functools.partial(fused, n), out_shape=(jax.ShapeDtypeStru...]
where the time goes in v2:
time: 126 us
  Pallas kernels  122 us (97%)
  local copies, waits for them, and re-layouts  2.96 us (2%)
    pallas_call x1, Pallas kernels, on_device_fused(): pl.pallas_call(functools.partial(fused, n), out_shape=(jax.ShapeDtypeStru...  122 us
    unnamed x2, local copies, waits for them, and re-layouts  2.96 us

profile of v2, /device:TPU:0, one launch (start us, length us, event | category | flops | bytes accessed | tf_op | source)
XLA Modules:
  0.0 125.7 jit_solution(10289352042869910667)
XLA Ops:
  0.6 122.1 %shard_map.104 = (bf16[320,512]{1,0:T(8,128)(2,1)}, f32[2,64]{1,0:T(2,128)}) custom-call(bf16[320,512]{1,0:T(8,128)(2,1)} %bitcast.12, bf16[320,512]{1,0:T(8,128)(2,1)} %bitcast.13, f32[1,5120]{1,0:T(1,128)} %bitcast.15, bf16[864,5120]{1,0:T(8,128)(2,1)} %bitcast.8, bf16[864,5120]{1,0:T(8,128)(2,1)} %bitcast.9, bf16[864,5120]{1,0:T(8,128)(2,1)} %w_down.1, ...), custom_call_target="tpu_custom_call" | custom-call | tf_op jit(solution)/shard_map/pallas_call | solution.py:618
  122.7 1.7 %copy.13 = bf16[512,320]{0,1:T(8,128)(2,1)} copy(bf16[512,320]{0,1:T(8,128)(2,1)} %bitcast.14) | data formatting | bytes 655360
  124.4 1.2 copy.14

commit v3 on v2

--- a/solution.py
+++ b/solution.py
@@ -246,7 +246,23 @@
         before_loop()
         for ch in range(CHUNKS):
             share(0, 0, ch, chip, 1 - core).wait_recv()
+        def pass_on(at, ch):
+            for direction in range(2):
+                q = chip_at(here - at) if direction == 0 else chip_at(here + at)
+                hop(direction, at, ch, q).wait_recv()
+
+                @pl.when(at < half - 1)
+                def _():
+                    hop(direction, at + 1, ch, q).start()
+
+                @pl.when((at == half - 1) & (core == direction))
+                def _():
+                    last_hop(direction, ch, q).start()
+
+                share(direction, at, ch, q, core).start()
+
         compute(chip)
+        pass_on(1, 0)
 
         @pl.loop(1, n)
         def _(i):
@@ -255,20 +271,12 @@
 
             @pl.when(odd & (at < half))
             def _():
-                for ch in range(CHUNKS):
-                    for direction in range(2):
-                        q = chip_at(here - at) if direction == 0 else chip_at(here + at)
-                        hop(direction, at, ch, q).wait_recv()
-
-                        @pl.when(at < half - 1)
-                        def _():
-                            hop(direction, at + 1, ch, q).start()
-
-                        @pl.when((at == half - 1) & (core == direction))
-                        def _():
-                            last_hop(direction, ch, q).start()
-
-                        share(direction, at, ch, q, core).start()
+                for ch in range(1, CHUNKS):
+                    pass_on(at, ch)
+
+            @pl.when(jnp.logical_not(odd) & (at + 1 < half))
+            def _():
+                pass_on(at + 1, 0)
 
             @pl.when(i == n - 1)
             def _():
@@ -552,7 +560,7 @@
         )
 
     zero = jnp.zeros((qs.shape[0], 2 * rank), F32)
-    sums = lax.fori_loop(0, tiles, add, (zero,) * seqs)
+    sums = lax.fori_loop(0, tiles, add, (zero,) * seqs, unroll=8)
     ones = jnp.ones((8, 2 * rank), F32)
     for s in range(seqs):
         scores[s : s + 1, :] = matmul_nt(ones, sums[s], HIGH)[0:1, :]

time: 126 us -> 124 us (0.984)
  Pallas kernels: 122 us -> 120 us
    pallas_call x1, Pallas kernels: 122 us -> 120 us  [on_device_fused(): pl.pallas_call(functools.partial(fused, n), out_shape=(jax.ShapeDtypeStru...]
where the time goes in v3:
time: 124 us
  Pallas kernels  120 us (97%)
  local copies, waits for them, and re-layouts  2.96 us (2%)
    pallas_call x1, Pallas kernels, on_device_fused(): pl.pallas_call(functools.partial(fused, n), out_shape=(jax.ShapeDtypeStru...  120 us
    unnamed x2, local copies, waits for them, and re-layouts  2.96 us

profile of v3, /device:TPU:0, one launch (start us, length us, event | category | flops | bytes accessed | tf_op | source)
XLA Modules:
  0.0 124.0 jit_solution(1760371646071220553)
XLA Ops:
  0.6 120.4 %shard_map.104 = (bf16[320,512]{1,0:T(8,128)(2,1)}, f32[2,64]{1,0:T(2,128)}) custom-call(bf16[320,512]{1,0:T(8,128)(2,1)} %bitcast.12, bf16[320,512]{1,0:T(8,128)(2,1)} %bitcast.13, f32[1,5120]{1,0:T(1,128)} %bitcast.15, bf16[864,5120]{1,0:T(8,128)(2,1)} %bitcast.8, bf16[864,5120]{1,0:T(8,128)(2,1)} %bitcast.9, bf16[864,5120]{1,0:T(8,128)(2,1)} %w_down.1, ...), custom_call_target="tpu_custom_call" | custom-call | tf_op jit(solution)/shard_map/pallas_call | solution.py:626
  121.0 1.7 %copy.13 = bf16[512,320]{0,1:T(8,128)(2,1)} copy(bf16[512,320]{0,1:T(8,128)(2,1)} %bitcast.14) | data formatting | bytes 655360
  122.7 1.2 %copy.14 = f32[2,64]{1,0:T(2,128)} copy(f32[2,64]{1,0:T(2,128)} %get-tuple-element.9) | data formatting | bytes 1024
